TPU v7x, 512 devices: a whole 4x8x8 slice. The times are simulated.
512 devices in a mesh: segment: 16 (over y, core), tile: 32 (over z, x).
Axes of the slice: x: 4, y: 8, z: 8, core: 2. Of those that a mesh axis runs over, the one named last changes fastest.
Arguments:
- tile_mask_amplitude: bfloat16 [512, 256, 256], P('tile', 'segment'), may hold values from -4 to 4
- tile_target_images: bfloat16 [512, 256, 256], P('tile', 'segment'), may hold values from 0 to 1
- spectra: float32 [12, 2, 31, 31], replicated, may hold values from -6 to 6
- slot_dose_scale: float32 [512], P('tile'), may hold values from 0.5 to 2
- slot_row: int32 [512], P('tile'), may hold values from -1 to 31, as said below
- side_source: int32 [512, 2], P('tile'), may hold values from -1 to 11, as said below
Outputs:
- corrected_mask: bfloat16 [512, 256, 256], P('tile', 'segment')
- resist_image: float32 [512, 256, 256], P('tile', 'segment')
Inputs may be any that keep to these rules, and one draw needn't show every extreme that they name: `slot_row`: in each tile owner's 16 slots the patterned tiles come first, with strictly rising tile rows below 32, and -1 marks the empty slots after them; every owner has at least 4 patterned tiles and at most 12, and some owner has exactly 12; every owner holds tile row 31. `side_source`: an entry names the slot of the neighbouring tile owner that holds the same tile row as this slot; it is -1 for empty slots, at the window's ends and where that tile is not patterned.
All inputs are finite; a program needn't handle non-finite values.
Results may differ from a plain program's by a relative error of at most 0.0075.
Values may be sent and summed in bfloat16 or wider, within the bound.
No kernel may reach another device: no remote copies, remote signals or barrier semaphores. Data moves between devices by JAX's collectives and lax.ppermute only.
A program may use at most 64 MiB of HBM per device.

v0:
```python
import math
import jax
import jax.numpy as jnp
from jax import lax
from jax.sharding import PartitionSpec as P

RB = 8
ITERS = 2
STEEPNESS = 1.5
THRESHOLD = 2.0
STEP_GAIN = 0.5


def passed_along(block, axis, distance):
    devices = range(lax.axis_size(axis))
    route = [(i - distance, i) for i in devices if i - distance in devices]
    return lax.ppermute(block, axis, route)


def with_halo(cells, sides, width):
    for axis, dim in sides:
        count = lax.axis_size(axis)
        head = lax.slice_in_dim(cells, 0, width, axis=dim)
        tail = lax.slice_in_dim(cells, cells.shape[dim] - width, cells.shape[dim], axis=dim)
        cells = jnp.concatenate(
            [
                lax.ppermute(tail, axis, [(i, (i + 1) % count) for i in range(count)]),
                cells,
                lax.ppermute(head, axis, [((i + 1) % count, i) for i in range(count)]),
            ],
            axis=dim,
        )
    return cells


def wave_tables(length, freq_count):
    position = jnp.arange(length, dtype=jnp.int32)
    frequency = jnp.arange(freq_count, dtype=jnp.int32) - freq_count // 2
    phase_index = position[:, None] * frequency[None, :] % length
    angle_rad = phase_index.astype(jnp.float32) * jnp.float32(2.0 * math.pi / length)
    return (jnp.cos(angle_rad), jnp.sin(angle_rad))


def transform_tables(length, freq_count):
    cosine, sine_part = wave_tables(length, freq_count)
    norm_scale = jnp.float32(1.0 / math.sqrt(length))
    forward_cols = jnp.concatenate([cosine * norm_scale, -(sine_part * norm_scale)], 1).astype(
        jnp.bfloat16
    )
    forward_rows = jnp.concatenate([cosine * norm_scale, sine_part * norm_scale], 1).astype(
        jnp.bfloat16
    )
    inverse_rows = jnp.concatenate([cosine, sine_part], 1).astype(jnp.bfloat16)
    cosine_low = cosine.T.astype(jnp.bfloat16)
    sine_low = sine_part.T.astype(jnp.bfloat16)
    inverse_cols = jnp.concatenate(
        [jnp.concatenate([cosine_low, sine_low], 1), jnp.concatenate([-sine_low, cosine_low], 1)], 0
    )
    return (forward_cols, forward_rows, inverse_rows, inverse_cols)


def blur_weights(radius):
    offsets = jnp.arange(2 * radius + 1, dtype=jnp.float32) - radius
    spread_width = radius / 2.0
    weights = jnp.exp(-offsets * offsets / (2.0 * spread_width * spread_width))
    return weights / jnp.sum(weights)


def spectrum_part(tile_rows, rows_table, forward_cols, freq_count):
    y_part = jnp.einsum(
        "nry,yb->nrb", tile_rows, forward_cols, preferred_element_type=jnp.float32
    ).astype(jnp.bfloat16)
    inner = jnp.einsum("ra,nrb->nab", rows_table, y_part, preferred_element_type=jnp.float32)
    real_part = inner[:, :freq_count, :freq_count] + inner[:, freq_count:, freq_count:]
    imag_part = inner[:, :freq_count, freq_count:] - inner[:, freq_count:, :freq_count]
    return jnp.stack([real_part, imag_part], 1)


def intensity_rows(spectrum, spectra, rows_inverse, inverse_cols, tile_edge):
    item_count = spectrum.shape[0]
    row_count = rows_inverse.shape[0]
    freq_count = spectra.shape[2]
    kernel_count = spectra.shape[0]
    block_len = 8
    spec_real = spectra[:, 0]
    spec_imag = spectra[:, 1]

    def one_block(spec_block):
        mask_real = spec_block[:, None, 0]
        mask_imag = spec_block[:, None, 1]
        prod_real = (spec_real * mask_real - spec_imag * mask_imag).astype(jnp.bfloat16)
        prod_imag = (spec_real * mask_imag + spec_imag * mask_real).astype(jnp.bfloat16)
        right_block = jnp.concatenate(
            [
                jnp.concatenate([prod_real, prod_imag], 3),
                jnp.concatenate([-prod_imag, prod_real], 3),
            ],
            2,
        )
        field_a = jnp.einsum(
            "ra,nkab->nkrb", rows_inverse, right_block, preferred_element_type=jnp.float32
        )
        field_a = (field_a * jnp.float32(1.0 / freq_count)).astype(jnp.bfloat16)
        field_full = jnp.einsum(
            "nkrb,by->nkry", field_a, inverse_cols, preferred_element_type=jnp.float32
        )
        squares = jnp.sum(field_full * field_full, axis=1)
        return (squares[..., :tile_edge] + squares[..., tile_edge:]) * jnp.float32(
            1.0 / kernel_count
        )

    grouped = spectrum.reshape(item_count // block_len, block_len, 2, freq_count, freq_count)
    return lax.map(one_block, grouped).reshape(item_count, row_count, tile_edge)


def pick_bands(received, source):
    valid = (source >= 0).astype(jnp.float32)
    taken = jnp.take(received, jnp.maximum(source, 0), axis=0)
    return taken * valid[:, None, None]


def body(tile_mask_amplitude, tile_target_images, spectra, slot_dose_scale, slot_row, side_source):
    slot_count, row_count, tile_edge = tile_mask_amplitude.shape
    freq_count = spectra.shape[2]
    segment_index = lax.axis_index("segment")
    last_segment = lax.axis_size("segment") - 1
    forward_cols, forward_rows, inverse_rows, inverse_cols = transform_tables(tile_edge, freq_count)
    rows_inverse = lax.dynamic_slice_in_dim(inverse_rows, segment_index * row_count, row_count, 0)
    weights = blur_weights(RB)
    weight = slot_dose_scale * (slot_row >= 0).astype(jnp.float32)
    slot_index = jnp.arange(slot_count, dtype=jnp.int32)
    prev_row = jnp.concatenate([jnp.full((1,), -7, jnp.int32), slot_row[:-1]])
    up_ok = (slot_index > 0) & (prev_row >= 0) & (slot_row >= 0) & (prev_row == slot_row - 1)
    down_ok = jnp.concatenate([up_ok[1:], jnp.zeros((1,), dtype=bool)])
    up_weight = up_ok.astype(jnp.float32)[:, None, None]
    down_weight = down_ok.astype(jnp.float32)[:, None, None]
    zero_rim = jnp.zeros((1, RB, tile_edge), jnp.float32)
    mask_now = tile_mask_amplitude
    resist = jnp.zeros((slot_count, row_count, tile_edge), jnp.float32)
    for sweep in range(ITERS):
        work_tiles = mask_now
        whole_tiles = lax.all_gather(work_tiles, "segment", axis=1, tiled=True)
        spectrum = spectrum_part(whole_tiles, forward_rows, forward_cols, freq_count)
        intensity = intensity_rows(spectrum, spectra, rows_inverse, inverse_cols, tile_edge)
        intensity = intensity * weight[:, None, None]
        from_left = passed_along(intensity[:, :, tile_edge - RB :], "tile", 1)
        from_right = passed_along(intensity[:, :, :RB], "tile", -1)
        left_band = pick_bands(from_left, side_source[:, 0])
        right_band = pick_bands(from_right, side_source[:, 1])
        padded = jnp.concatenate([left_band, intensity, right_band], 2)
        horiz_blur = weights[0] * padded[:, :, 0:tile_edge]
        for shift_by in range(1, 2 * RB + 1):
            horiz_blur = (
                horiz_blur + weights[shift_by] * padded[:, :, shift_by : shift_by + tile_edge]
            )
        extended = with_halo(horiz_blur.astype(jnp.bfloat16), (("segment", 1),), RB).astype(
            horiz_blur.dtype
        )
        upper_rim = extended[:, :RB]
        lower_rim = extended[:, row_count + RB :]
        upper_next = jnp.concatenate([zero_rim, upper_rim[:-1]], 0) * up_weight
        lower_next = jnp.concatenate([lower_rim[1:], zero_rim], 0) * down_weight
        upper_rim = jnp.where(segment_index == 0, upper_next, upper_rim)
        lower_rim = jnp.where(segment_index == last_segment, lower_next, lower_rim)
        vert_padded = jnp.concatenate([upper_rim, horiz_blur, lower_rim], 1)
        vert_blur = weights[0] * vert_padded[:, 0:row_count, :]
        for shift_by in range(1, 2 * RB + 1):
            vert_blur = (
                vert_blur + weights[shift_by] * vert_padded[:, shift_by : shift_by + row_count, :]
            )
        resist = jax.nn.sigmoid(STEEPNESS * (vert_blur - THRESHOLD))
        mask_now = (
            mask_now.astype(jnp.float32)
            + STEP_GAIN * (tile_target_images.astype(jnp.float32) - resist)
        ).astype(jnp.bfloat16)
    return (mask_now, resist)


def solution(mesh):
    in_specs = (
        P("tile", "segment", None),
        P("tile", "segment", None),
        P(),
        P("tile"),
        P("tile"),
        P("tile", None),
    )
    out_specs = (P("tile", "segment", None), P("tile", "segment", None))
    return jax.shard_map(body, mesh=mesh, in_specs=in_specs, out_specs=out_specs, check_vma=False)
```

profile of v0, /device:TPU:199, one launch (start us, length us, event | category | flops | bytes accessed | tf_op | source)
XLA Modules:
  0.0 219.9 jit_solution(1284356911872364960)
XLA Ops:
  16.5 38.4 %all-gather.3.cloned.1.call-done = bf16[16,256,256]{2,1,0:T(8,128)(2,1)} async-done(((bf16[16,16,256]{2,1,0:T(8,128)(2,1)}), bf16[16,256,256]{2,1,0:T(8,128)(2,1)}) %all-gather.3.cloned.1.call-update) | async-done | bytes 2097168 | tf_op jit(solution)/shard_map/all_gather | solution.py:142
  55.0 2.5 %fusion.67 = f32[16,62,62]{1,2,0:T(8,128)S(1)} fusion(bf16[16,256,256]{2,1,0:T(8,128)(2,1)} %all-gather.3.cloned.1.call-done, bf16[256,31]{0,1:T(8,128)(2,1)S(1)} %get-tuple-element.236, bf16[256,31]{0,1:T(8,128)(2,1)S(1)} %get-tuple-element.234, bf16[256,31]{0,1:T(8,128)(2,1)S(1)} %get-tuple-element.235), kind=kOutput, calls=%fused_computation.64 | convolution fusion | flops 161894400 | bytes 2390784 | tf_op jit(solution)/shard_map/ra,nrb->nab/dot_general | solution.py:73
  58.9 8.2 %while.20 = (s32[]{:T(128)}, f32[2,8,16,256]{3,2,1,0:T(8,128)}, f32[12,1,31,31]{3,2,0,1:T(8,128)S(1)}, f32[2,8,2,31,31]{4,1,3,2,0:T(8,128)S(1)}, f32[12,1,31,31]...) while((s32[]{:T(128)}, f32[2,8,16,256]{3,2,1,0:T(8,128)}, ...), condition=%wide.region_3.4_spmd, body=%wide.region_1.3_spmd.sunk | while | flops 115241184 | bytes 2505049 | solution.py:113
  59.7 2.6 %multiply_reduce_fusion.4 = f32[8,16,512]{2,1,0:T(8,128)S(1)} fusion(bf16[8,12,31,31]{3,2,1,0:T(8,128)(2,1)S(1)} %get-tuple-element.326, bf16[8,12,31,31]{3,2,1,0:T(8,128)(2,1)S(1)} %fusion.337, bf16[8,12,31,31]{3,2,1,0:T(8,128)(2,1)S(1)} %get-tuple-element.327, bf16[62,512]{1,0:T(8,128)(2,1)} %get-tuple-element.361, ...), kind=kOutput, calls=%fused_computation.4.clone.1 | convolution fusion | flops 113976320 | bytes 881152 | tf_op jit(solution)/shard_map/while/body/eval_jaxpr/nkrb,by->nkry/dot_general | solution.py:104
  63.8 2.6 %multiply_reduce_fusion.4 = f32[8,16,512]{2,1,0:T(8,128)S(1)} fusion(bf16[8,12,31,31]{3,2,1,0:T(8,128)(2,1)S(1)} %get-tuple-element.326, bf16[8,12,31,31]{3,2,1,0:T(8,128)(2,1)S(1)} %fusion.337, bf16[8,12,31,31]{3,2,1,0:T(8,128)(2,1)S(1)} %get-tuple-element.327, bf16[62,512]{1,0:T(8,128)(2,1)} %get-tuple-element.361, ...), kind=kOutput, calls=%fused_computation.4.clone.1 | convolution fusion | flops 113976320 | bytes 881152 | tf_op jit(solution)/shard_map/while/body/eval_jaxpr/nkrb,by->nkry/dot_general | solution.py:104
  68.2 4.5 %collective-permute-start = (f32[16,16,8]{2,1,0:T(8,128)S(1)}, f32[16,16,8]{2,1,0:T(8,128)S(1)}, u32[]{:S(2)}, u32[]{:S(2)}) collective-permute-start(f32[16,16,8]{2,1,0:T(8,128)S(1)} %get-tuple-element.203), channel_id=1, source_target_pairs={{0,1},{1,2},{2,3},{3,4},{4,5},{5,6},{6,7},{7,8},{8,9},{9,10},{10,1... | collective-permute-start | bytes 24584 | tf_op jit(solution)/shard_map/ppermute | solution.py:17
  74.1 2.1 collective-permute-start.1
  77.9 5.9 %collective-permute-done.1 = f32[16,16,8]{2,1,0:T(8,128)S(1)} collective-permute-done((f32[16,16,8]{2,1,0:T(8,128)S(1)}, f32[16,16,8]{2,1,0:T(8,128)S(1)}, u32[]{:S(2)}, u32[]{:S(2)}) %collective-permute-start.1) | collective-permute-done | bytes 8224 | tf_op jit(solution)/shard_map/ppermute | solution.py:17
  84.5 12.2 %fusion.315 = (bf16[16,16,256]{2,1,0:T(8,128)(2,1)S(1)}, f32[16,16,256]{2,1,0:T(8,128)S(1)}) fusion(f32[16,16,8]{2,1,0:T(8,128)S(1)} %select_multiply_fusion.1, f32[16,16,256]{2,1,0:T(8,128)S(1)} %bitcast_multiply_fusion.1, f32[]{:T(128)} %bitcast.49, f32[]{:T(128)} %bitcast.48, f32[]{:T(128)} %bitcast.47, f32[]{:T(128)} %bitcast.46, f32[]{:T(128)} %bitcast.45, ...), kind=kLoop, calls=%fused_computation.474 | loop fusion | flops 3276800 | bytes 671812 | tf_op jit(solution)/shard_map/convert_element_type | solution.py:156
  96.7 2.2 collective-permute-start.2
  100.2 2.4 %collective-permute-done.3 = bf16[16,8,256]{2,1,0:T(8,128)(2,1)S(1)} collective-permute-done((bf16[16,8,256]{2,1,0:T(8,128)(2,1)S(1)}, bf16[16,8,256]{2,1,0:T(8,128)(2,1)S(1)}, u32[]{:S(2)}, u32[]{:S(2)}) %collective-permute-start.3) | collective-permute-done | bytes 65568 | tf_op jit(solution)/shard_map/ppermute | solution.py:29
  102.8 11.4 %fusion.76 = bf16[16,16,256]{2,1,0:T(8,128)(2,1)S(1)} fusion(bf16[16,16,256]{2,1,0:T(8,128)(2,1)S(1)} %copy-done.2, f32[16,16,256]{2,1,0:T(8,128)S(1)} %get-tuple-element.174, f32[16,8,256]{2,1,0:T(8,128)S(1)} %get-tuple-element.200, f32[16,8,256]{2,1,0:T(8,128)S(1)} %get-tuple-element.199, bf16[16,16,256]{2,1,0:T(8,128)(2,1)S(1)} %copy-done.4, ...), kind=kLoop, calls=%fused_computation.185 | loop fusion | flops 3932160 | bytes 917572 | tf_op jit(solution)/shard_map/convert_element_type | solution.py:175
  115.6 38.8 %all-gather.5.cloned.1.call-done = bf16[16,256,256]{2,0,1:T(8,128)(2,1)} async-done(((bf16[16,16,256]{2,0,1:T(8,128)(2,1)}), bf16[16,256,256]{2,0,1:T(8,128)(2,1)}) %all-gather.5.cloned.1.call-update) | async-done | bytes 2097168 | tf_op jit(solution)/shard_map/all_gather | solution.py:142
  154.4 2.5 %fusion.71 = f32[16,62,62]{1,2,0:T(8,128)S(1)} fusion(bf16[16,256,256]{2,0,1:T(8,128)(2,1)} %all-gather.5.cloned.1.call-done, bf16[256,31]{0,1:T(8,128)(2,1)S(1)} %get-tuple-element.236, bf16[256,31]{0,1:T(8,128)(2,1)S(1)} %get-tuple-element.234, bf16[256,31]{0,1:T(8,128)(2,1)S(1)} %copy-done.6), kind=kOutput, calls=%fused_computation.66 | convolution fusion | flops 161894400 | bytes 2390784 | tf_op jit(solution)/shard_map/ra,nrb->nab/dot_general | solution.py:73
  158.4 8.2 %while.21 = (s32[]{:T(128)}, f32[2,8,16,256]{3,2,1,0:T(8,128)}, f32[12,1,31,31]{3,2,0,1:T(8,128)S(1)}, f32[2,8,2,31,31]{4,1,3,2,0:T(8,128)S(1)}, f32[12,1,31,31]...) while((s32[]{:T(128)}, f32[2,8,16,256]{3,2,1,0:T(8,128)}, ...), condition=%wide.region_6.8_spmd, body=%wide.region_4.7_spmd.sunk | while | flops 115241184 | bytes 2505049 | solution.py:113
  159.2 2.6 %multiply_reduce_fusion.5 = f32[8,16,512]{2,1,0:T(8,128)S(1)} fusion(bf16[8,12,31,31]{3,2,1,0:T(8,128)(2,1)S(1)} %get-tuple-element.337, bf16[8,12,31,31]{3,2,1,0:T(8,128)(2,1)S(1)} %fusion.342, bf16[8,12,31,31]{3,2,1,0:T(8,128)(2,1)S(1)} %get-tuple-element.338, bf16[62,512]{1,0:T(8,128)(2,1)} %get-tuple-element.385, ...), kind=kOutput, calls=%fused_computation.31.clone.1 | convolution fusion | flops 113976320 | bytes 881152 | tf_op jit(solution)/shard_map/while/body/eval_jaxpr/nkrb,by->nkry/dot_general | solution.py:104
  163.3 2.6 %multiply_reduce_fusion.5 = f32[8,16,512]{2,1,0:T(8,128)S(1)} fusion(bf16[8,12,31,31]{3,2,1,0:T(8,128)(2,1)S(1)} %get-tuple-element.337, bf16[8,12,31,31]{3,2,1,0:T(8,128)(2,1)S(1)} %fusion.342, bf16[8,12,31,31]{3,2,1,0:T(8,128)(2,1)S(1)} %get-tuple-element.338, bf16[62,512]{1,0:T(8,128)(2,1)} %get-tuple-element.385, ...), kind=kOutput, calls=%fused_computation.31.clone.1 | convolution fusion | flops 113976320 | bytes 881152 | tf_op jit(solution)/shard_map/while/body/eval_jaxpr/nkrb,by->nkry/dot_general | solution.py:104
  167.8 4.5 %collective-permute-start.4 = (f32[16,16,8]{2,1,0:T(8,128)S(1)}, f32[16,16,8]{2,1,0:T(8,128)S(1)}, u32[]{:S(2)}, u32[]{:S(2)}) collective-permute-start(f32[16,16,8]{2,1,0:T(8,128)S(1)} %get-tuple-element.197), channel_id=1, source_target_pairs={{0,1},{1,2},{2,3},{3,4},{4,5},{5,6},{6,7},{7,8},{8,9},{9,10},{10,1... | collective-permute-start | bytes 24584 | tf_op jit(solution)/shard_map/ppermute | solution.py:17
  172.2 1.9 collective-permute-start.5
  175.9 6.1 %collective-permute-done.5 = f32[16,16,8]{2,1,0:T(8,128)S(1)} collective-permute-done((f32[16,16,8]{2,1,0:T(8,128)S(1)}, f32[16,16,8]{2,1,0:T(8,128)S(1)}, u32[]{:S(2)}, u32[]{:S(2)}) %collective-permute-start.5) | collective-permute-done | bytes 8224 | tf_op jit(solution)/shard_map/ppermute | solution.py:17
  182.7 12.2 %fusion.312 = (bf16[16,16,256]{2,1,0:T(8,128)(2,1)S(1)}, f32[16,16,256]{2,1,0:T(8,128)S(1)}) fusion(f32[16,16,8]{2,1,0:T(8,128)S(1)} %select_multiply_fusion, f32[16,16,256]{2,1,0:T(8,128)S(1)} %bitcast_multiply_fusion, f32[]{:T(128)} %bitcast.49, f32[]{:T(128)} %bitcast.48, f32[]{:T(128)} %bitcast.47, f32[]{:T(128)} %bitcast.46, f32[]{:T(128)} %bitcast.45, ...), kind=kLoop, calls=%fused_computation.472 | loop fusion | flops 3276800 | bytes 671812 | tf_op jit(solution)/shard_map/convert_element_type | solution.py:156
  194.9 2.1 collective-permute-start.6
  198.4 2.4 %collective-permute-done.7 = bf16[16,8,256]{2,1,0:T(8,128)(2,1)S(1)} collective-permute-done((bf16[16,8,256]{2,1,0:T(8,128)(2,1)S(1)}, bf16[16,8,256]{2,1,0:T(8,128)(2,1)S(1)}, u32[]{:S(2)}, u32[]{:S(2)}) %collective-permute-start.7) | collective-permute-done | bytes 65568 | tf_op jit(solution)/shard_map/ppermute | solution.py:29
  201.0 12.1 %fusion.79 = (bf16[16,16,256]{2,1,0:T(8,128)(2,1)}, f32[16,16,256]{2,1,0:T(8,128)}) fusion(bf16[16,16,256]{2,1,0:T(8,128)(2,1)S(1)} %copy-done.3, bf16[16,16,256]{2,1,0:T(8,128)(2,1)S(1)} %copy-done.1, f32[16,8,256]{2,1,0:T(8,128)S(1)} %get-tuple-element.194, f32[16,16,256]{2,1,0:T(8,128)S(1)} %get-tuple-element.170, f32[]{:T(128)} %bitcast.49, ...), kind=kLoop, calls=%fused_computation.188 | loop fusion | flops 3932160 | bytes 1179716 | tf_op jit(solution)/shard_map/convert_element_type | solution.py:175
  (130 shorter events, 30.5 us)
Async XLA Ops:
  7.2 47.8 %all-gather.3.cloned.1.call-start = ((), (), s32[]{:S(2)}) async-start(), calls=%async_computation | async-start | bytes 2228224 | tf_op jit(solution)/shard_map/all_gather | solution.py:142
  7.9 146.5 %all-gather.5.cloned.1.call-start = ((), (), s32[]{:S(2)}) async-start(), calls=%async_computation.1 | async-start | bytes 2228224 | tf_op jit(solution)/shard_map/all_gather | solution.py:142
  8.2 46.8 %copy-start.5 = (bf16[256,31]{0,1:T(8,128)(2,1)}, bf16[256,31]{0,1:T(8,128)(2,1)S(1)}, u32[]{:S(2)}) copy-start(bf16[256,31]{0,1:T(8,128)(2,1)S(1)} %get-tuple-element.235) | copy-start | bytes 47620
  67.1 17.3 %copy-start.8 = (pred[16]{0:T(512)(128)(4,1)S(1)}, pred[16]{0:T(512)(128)(4,1)}, u32[]{:S(2)}) copy-start(pred[16]{0:T(512)(128)(4,1)} %get-tuple-element.211) | copy-start | bytes 52
  67.1 17.3 %copy-start.10 = (f32[16]{0:T(128)S(1)}, f32[16]{0:T(128)}, u32[]{:S(2)}) copy-start(f32[16]{0:T(128)} %get-tuple-element.210) | copy-start | bytes 196
  68.2 34.5 %copy-start.7 = (f32[16]{0:T(128)S(1)}, f32[16]{0:T(128)}, u32[]{:S(2)}) copy-start(f32[16]{0:T(128)} %get-tuple-element.171) | copy-start | bytes 196
  68.2 8.0 %collective-permute-start = (f32[16,16,8]{2,1,0:T(8,128)S(1)}, f32[16,16,8]{2,1,0:T(8,128)S(1)}, u32[]{:S(2)}, u32[]{:S(2)}) collective-permute-start(f32[16,16,8]{2,1,0:T(8,128)S(1)} %get-tuple-element.203), channel_id=1, source_target_pairs={{0,1},{1,2},{2,3},{3,4},{4,5},{5,6},{6,7},{7,8},{8,9},{9,10},{10,1... | collective-permute-start | bytes 24584 | tf_op jit(solution)/shard_map/ppermute | solution.py:17
  74.1 9.7 %collective-permute-start.1 = (f32[16,16,8]{2,1,0:T(8,128)S(1)}, f32[16,16,8]{2,1,0:T(8,128)S(1)}, u32[]{:S(2)}, u32[]{:S(2)}) collective-permute-start(f32[16,16,8]{2,1,0:T(8,128)S(1)} %get-tuple-element.204), channel_id=1, source_target_pairs={{1,0},{2,1},{3,2},{4,3},{5,4},{6,5},{7,6},{8,7},{9,8},{10,9},{11,1... | collective-permute-start | bytes 24584 | tf_op jit(solution)/shard_map/ppermute | solution.py:17
  77.8 25.0 %copy-start.2 = (bf16[16,16,256]{2,1,0:T(8,128)(2,1)S(1)}, bf16[16,16,256]{2,1,0:T(8,128)(2,1)}, u32[]{:S(2)}) copy-start(bf16[16,16,256]{2,1,0:T(8,128)(2,1)} %param.13) | copy-start | bytes 393220
  77.9 25.0 %copy-start.4 = (bf16[16,16,256]{2,1,0:T(8,128)(2,1)S(1)}, bf16[16,16,256]{2,1,0:T(8,128)(2,1)}, u32[]{:S(2)}) copy-start(bf16[16,16,256]{2,1,0:T(8,128)(2,1)} %param.12) | copy-start | bytes 393220
  96.7 57.7 %copy-start.6 = (bf16[256,31]{0,1:T(8,128)(2,1)S(1)}, bf16[256,31]{0,1:T(8,128)(2,1)}, u32[]{:S(2)}) copy-start(bf16[256,31]{0,1:T(8,128)(2,1)} %copy-done.5) | copy-start | bytes 47620
  96.7 3.5 %collective-permute-start.2 = (bf16[16,8,256]{2,1,0:T(8,128)(2,1)S(1)}, bf16[16,8,256]{2,1,0:T(8,128)(2,1)S(1)}, u32[]{:S(2)}, u32[]{:S(2)}) collective-permute-start(bf16[16,8,256]{2,1,0:T(8,128)(2,1)S(1)} %get-tuple-element.207), channel_id=1, source_target_pairs={{0,32},{32,64},{64,96},{96,128},{128,160},{160,192},{192,224},{224... | collective-permute-start | bytes 196616 | tf_op jit(solution)/shard_map/ppermute | solution.py:27
  98.9 3.8 %collective-permute-start.3 = (bf16[16,8,256]{2,1,0:T(8,128)(2,1)S(1)}, bf16[16,8,256]{2,1,0:T(8,128)(2,1)S(1)}, u32[]{:S(2)}, u32[]{:S(2)}) collective-permute-start(bf16[16,8,256]{2,1,0:T(8,128)(2,1)S(1)} %get-tuple-element.208), channel_id=1, source_target_pairs={{32,0},{64,32},{96,64},{128,96},{160,128},{192,160},{224,192},{256... | collective-permute-start | bytes 196616 | tf_op jit(solution)/shard_map/ppermute | solution.py:29
  99.0 58.0 %copy-start.15 = (f32[16]{0:T(128)}, f32[16]{0:T(128)S(1)}, u32[]{:S(2)}) copy-start(f32[16]{0:T(128)S(1)} %add_convert_fusion.2) | copy-start | bytes 196
  158.4 8.2 %copy-start.14 = (f32[16]{0:T(128)S(1)}, f32[16]{0:T(128)}, u32[]{:S(2)}) copy-start(f32[16]{0:T(128)} %compare_select_fusion.2) | copy-start | bytes 196
  158.4 17.3 %copy-start.9 = (pred[16]{0:T(512)(128)(4,1)S(1)}, pred[16]{0:T(512)(128)(4,1)}, u32[]{:S(2)}) copy-start(pred[16]{0:T(512)(128)(4,1)} %get-tuple-element.175) | copy-start | bytes 52
  158.4 17.3 %copy-start.11 = (f32[16]{0:T(128)S(1)}, f32[16]{0:T(128)}, u32[]{:S(2)}) copy-start(f32[16]{0:T(128)} %get-tuple-element.209) | copy-start | bytes 196
  167.7 33.1 %copy-start.16 = (f32[16]{0:T(128)S(1)}, f32[16]{0:T(128)}, u32[]{:S(2)}) copy-start(f32[16]{0:T(128)} %copy-done.15) | copy-start | bytes 196
  167.8 7.1 %collective-permute-start.4 = (f32[16,16,8]{2,1,0:T(8,128)S(1)}, f32[16,16,8]{2,1,0:T(8,128)S(1)}, u32[]{:S(2)}, u32[]{:S(2)}) collective-permute-start(f32[16,16,8]{2,1,0:T(8,128)S(1)} %get-tuple-element.197), channel_id=1, source_target_pairs={{0,1},{1,2},{2,3},{3,4},{4,5},{5,6},{6,7},{7,8},{8,9},{9,10},{10,1... | collective-permute-start | bytes 24584 | tf_op jit(solution)/shard_map/ppermute | solution.py:17
  172.2 9.7 %collective-permute-start.5 = (f32[16,16,8]{2,1,0:T(8,128)S(1)}, f32[16,16,8]{2,1,0:T(8,128)S(1)}, u32[]{:S(2)}, u32[]{:S(2)}) collective-permute-start(f32[16,16,8]{2,1,0:T(8,128)S(1)} %get-tuple-element.198), channel_id=1, source_target_pairs={{1,0},{2,1},{3,2},{4,3},{5,4},{6,5},{7,6},{8,7},{9,8},{10,9},{11,1... | collective-permute-start | bytes 24584 | tf_op jit(solution)/shard_map/ppermute | solution.py:17
  175.8 25.1 %copy-start.1 = (bf16[16,16,256]{2,1,0:T(8,128)(2,1)S(1)}, bf16[16,16,256]{2,1,0:T(8,128)(2,1)}, u32[]{:S(2)}) copy-start(bf16[16,16,256]{2,1,0:T(8,128)(2,1)} %copy-done) | copy-start | bytes 393220
  175.8 25.1 %copy-start.3 = (bf16[16,16,256]{2,1,0:T(8,128)(2,1)S(1)}, bf16[16,16,256]{2,1,0:T(8,128)(2,1)}, u32[]{:S(2)}) copy-start(bf16[16,16,256]{2,1,0:T(8,128)(2,1)} %param.13) | copy-start | bytes 393220
  194.9 3.5 %collective-permute-start.6 = (bf16[16,8,256]{2,1,0:T(8,128)(2,1)S(1)}, bf16[16,8,256]{2,1,0:T(8,128)(2,1)S(1)}, u32[]{:S(2)}, u32[]{:S(2)}) collective-permute-start(bf16[16,8,256]{2,1,0:T(8,128)(2,1)S(1)} %get-tuple-element.205), channel_id=1, source_target_pairs={{0,32},{32,64},{64,96},{96,128},{128,160},{160,192},{192,224},{224... | collective-permute-start | bytes 196616 | tf_op jit(solution)/shard_map/ppermute | solution.py:27
  197.0 3.8 %collective-permute-start.7 = (bf16[16,8,256]{2,1,0:T(8,128)(2,1)S(1)}, bf16[16,8,256]{2,1,0:T(8,128)(2,1)S(1)}, u32[]{:S(2)}, u32[]{:S(2)}) collective-permute-start(bf16[16,8,256]{2,1,0:T(8,128)(2,1)S(1)} %get-tuple-element.206), channel_id=1, source_target_pairs={{32,0},{64,32},{96,64},{128,96},{160,128},{192,160},{224,192},{256... | collective-permute-start | bytes 196616 | tf_op jit(solution)/shard_map/ppermute | solution.py:29
  (5 other events, 21.7 us)
Sparse Core Ops, SparseCore 0:
  10.2 44.7 all-gather.2
  115.7 38.6 all-gather.4
where the time goes:
time: 221 us; the launch traced here: 220 us
  waiting for transfers between devices  98.1 us (44%)
  other arithmetic  63.5 us (29%)
  starting transfers between devices  17.3 us (8%)
  matrix products  15.4 us (7%)
  between operations  14.5 us (7%)
  local copies, waits for them, and re-layouts  10.8 us (5%)
    all_gather x2, waiting for transfers between devices, body(): whole_tiles = lax.all_gather(work_tiles, 'segment', axis=1, tiled=True)  77.3 us
    convert_element_type x2, other arithmetic, body(): horiz_blur.astype(jnp.bfloat16)  24.4 us
    convert_element_type x2, other arithmetic, body(): mask_now = (mask_now.astype(jnp.float32) + STEP_GAIN * (tile_target_image...  23.5 us
    ppermute x4, starting transfers between devices, passed_along(): return lax.ppermute(block, axis, route)  13 us
    ppermute x4, waiting for transfers between devices, passed_along(): return lax.ppermute(block, axis, route)  12.7 us
    dot_general x4, matrix products, one_block(): jnp.einsum('nkrb,by->nkry', field_a, inverse_cols, preferred_element_type...  10.4 us
    dot_general x2, matrix products, spectrum_part(): jnp.einsum('ra,nrb->nab', rows_table, y_part, preferred_element_type=jnp....  5.01 us
    ppermute x2, waiting for transfers between devices, with_halo(): lax.ppermute(head, axis, [((i + 1) % count, i) for i in range(count)])  4.87 us
  transfers between devices with their start and end apart: 10, of which 9 were waited for; matrix products, arithmetic and copies ran while one was open for 6% of the time, Pallas kernels for 0%

commit v1 on v0

--- a/solution.py
+++ b/solution.py
@@ -9,6 +9,11 @@
 STEEPNESS = 1.5
 THRESHOLD = 2.0
 STEP_GAIN = 0.5
+
+
+def all_by_exchange(x, axis, dim):
+    outgoing = jnp.stack([x] * lax.axis_size(axis))
+    return jnp.concatenate(lax.all_to_all(outgoing, axis, 0, 0), axis=dim)
 
 
 def passed_along(block, axis, distance):
@@ -139,7 +144,7 @@
     resist = jnp.zeros((slot_count, row_count, tile_edge), jnp.float32)
     for sweep in range(ITERS):
         work_tiles = mask_now
-        whole_tiles = lax.all_gather(work_tiles, "segment", axis=1, tiled=True)
+        whole_tiles = all_by_exchange(work_tiles, "segment", 1)
         spectrum = spectrum_part(whole_tiles, forward_rows, forward_cols, freq_count)
         intensity = intensity_rows(spectrum, spectra, rows_inverse, inverse_cols, tile_edge)
         intensity = intensity * weight[:, None, None]

time: 221 us -> 233 us (1.054)
  the two profiles are of different devices: /device:TPU:199 before, /device:TPU:255 now
where the time goes in v1:
time: 233 us; the launch traced here: 231 us
  other arithmetic  63.6 us (27%)
  waiting for transfers between devices  59.7 us (26%)
  blocking collectives  51.5 us (22%)
  starting transfers between devices  28.1 us (12%)
  matrix products  13.8 us (6%)
  local copies, waits for them, and re-layouts  13.4 us (6%)
    all_to_all x1, blocking collectives, all_by_exchange(): return jnp.concatenate(lax.all_to_all(outgoing, axis, 0, 0), axis=dim)  51.5 us
    all_to_all x1, waiting for transfers between devices, all_by_exchange(): return jnp.concatenate(lax.all_to_all(outgoing, axis, 0, 0), axis=dim)  39.6 us
    convert_element_type x2, other arithmetic, body(): horiz_blur.astype(jnp.bfloat16)  24.4 us
    convert_element_type x2, other arithmetic, body(): mask_now = (mask_now.astype(jnp.float32) + STEP_GAIN * (tile_target_image...  23.5 us
    ppermute x4, starting transfers between devices, passed_along(): return lax.ppermute(block, axis, route)  12.3 us
    dot_general x4, matrix products, one_block(): jnp.einsum('nkrb,by->nkry', field_a, inverse_cols, preferred_element_type...  10.4 us
    ppermute x4, waiting for transfers between devices, passed_along(): return lax.ppermute(block, axis, route)  10.3 us
    ppermute x2, starting transfers between devices, with_halo(): lax.ppermute(tail, axis, [(i, (i + 1) % count) for i in range(count)])  8.44 us
  transfers between devices with their start and end apart: 9, of which 8 were waited for; matrix products, arithmetic and copies ran while one was open for 5% of the time, Pallas kernels for 0%

profile of v1, /device:TPU:255, one launch (start us, length us, event | category | flops | bytes accessed | tf_op | source)
XLA Modules:
  0.0 231.4 jit_solution(15164093756200010765)
XLA Ops:
  0.6 2.5 %stack.16 = bf16[16,16,16,256]{3,2,1,0:T(8,128)(2,1)} broadcast(bf16[16,16,256]{2,1,0:T(8,128)(2,1)} %param.12), dimensions={1,2,3} | broadcast | bytes 2228224 | tf_op jit(solution)/shard_map/stack | solution.py:15
  3.1 7.3 %all-to-all-start = ((bf16[16,16,16,256]{3,2,1,0:T(8,128)(2,1)}), bf16[16,16,16,256]{3,2,1,0:T(8,128)(2,1)S(1)}, u32[]{:S(2)}, u32[]{:S(2)}) async-start(bf16[16,16,16,256]{3,2,1,0:T(8,128)(2,1)} %stack.16), calls=%async_computation | async-start | bytes 4194304 | tf_op jit(solution)/shard_map/all_to_all | solution.py:16
  17.9 39.6 %all-to-all-done = bf16[16,16,16,256]{3,2,1,0:T(8,128)(2,1)S(1)} async-done(((bf16[16,16,16,256]{3,2,1,0:T(8,128)(2,1)}), bf16[16,16,16,256]{3,2,1,0:T(8,128)(2,1)S(1)}, u32[]{:S(2)}, u32[]{:S(2)}) %all-to-all-start) | async-done | bytes 2097184 | tf_op jit(solution)/shard_map/all_to_all | solution.py:16
  59.1 2.5 %fusion.62 = f32[16,62,62]{1,2,0:T(8,128)S(1)} fusion(bf16[16,256,256]{2,1,0:T(8,128)(2,1)} %bitcast.159, bf16[256,31]{0,1:T(8,128)(2,1)S(1)} %get-tuple-element.236, bf16[256,31]{0,1:T(8,128)(2,1)S(1)} %get-tuple-element.234, bf16[256,31]{0,1:T(8,128)(2,1)S(1)} %get-tuple-element.235), kind=kOutput, calls=%fused_computation.62 | convolution fusion | flops 161894400 | bytes 2390784 | tf_op jit(solution)/shard_map/ra,nrb->nab/dot_general | solution.py:78
  63.0 8.2 %while.20 = (s32[]{:T(128)}, f32[2,8,16,256]{3,2,1,0:T(8,128)}, f32[12,1,31,31]{3,2,0,1:T(8,128)S(1)}, f32[2,8,2,31,31]{4,1,3,2,0:T(8,128)S(1)}, f32[12,1,31,31]...) while((s32[]{:T(128)}, f32[2,8,16,256]{3,2,1,0:T(8,128)}, ...), condition=%wide.region_3.4_spmd, body=%wide.region_1.3_spmd.sunk | while | flops 115241184 | bytes 2505049 | solution.py:118
  63.8 2.6 %multiply_reduce_fusion.4 = f32[8,16,512]{2,1,0:T(8,128)S(1)} fusion(bf16[8,12,31,31]{3,2,1,0:T(8,128)(2,1)S(1)} %get-tuple-element.326, bf16[8,12,31,31]{3,2,1,0:T(8,128)(2,1)S(1)} %fusion.329, bf16[8,12,31,31]{3,2,1,0:T(8,128)(2,1)S(1)} %get-tuple-element.327, bf16[62,512]{1,0:T(8,128)(2,1)} %get-tuple-element.361, ...), kind=kOutput, calls=%fused_computation.4.clone.1 | convolution fusion | flops 113976320 | bytes 881152 | tf_op jit(solution)/shard_map/while/body/eval_jaxpr/nkrb,by->nkry/dot_general | solution.py:109
  67.9 2.6 %multiply_reduce_fusion.4 = f32[8,16,512]{2,1,0:T(8,128)S(1)} fusion(bf16[8,12,31,31]{3,2,1,0:T(8,128)(2,1)S(1)} %get-tuple-element.326, bf16[8,12,31,31]{3,2,1,0:T(8,128)(2,1)S(1)} %fusion.329, bf16[8,12,31,31]{3,2,1,0:T(8,128)(2,1)S(1)} %get-tuple-element.327, bf16[62,512]{1,0:T(8,128)(2,1)} %get-tuple-element.361, ...), kind=kOutput, calls=%fused_computation.4.clone.1 | convolution fusion | flops 113976320 | bytes 881152 | tf_op jit(solution)/shard_map/while/body/eval_jaxpr/nkrb,by->nkry/dot_general | solution.py:109
  72.4 5.1 %collective-permute-start = (f32[16,16,8]{2,1,0:T(8,128)S(1)}, f32[16,16,8]{2,1,0:T(8,128)S(1)}, u32[]{:S(2)}, u32[]{:S(2)}) collective-permute-start(f32[16,16,8]{2,1,0:T(8,128)S(1)} %get-tuple-element.203), channel_id=1, source_target_pairs={{0,1},{1,2},{2,3},{3,4},{4,5},{5,6},{6,7},{7,8},{8,9},{9,10},{10,1... | collective-permute-start | bytes 24584 | tf_op jit(solution)/shard_map/ppermute | solution.py:22
  82.5 5.4 %collective-permute-done.1 = f32[16,16,8]{2,1,0:T(8,128)S(1)} collective-permute-done((f32[16,16,8]{2,1,0:T(8,128)S(1)}, f32[16,16,8]{2,1,0:T(8,128)S(1)}, u32[]{:S(2)}, u32[]{:S(2)}) %collective-permute-start.1) | collective-permute-done | bytes 8224 | tf_op jit(solution)/shard_map/ppermute | solution.py:22
  88.6 12.2 %fusion.306 = (bf16[16,16,256]{2,1,0:T(8,128)(2,1)S(1)}, f32[16,16,256]{2,1,0:T(8,128)S(1)}) fusion(f32[16,16,8]{2,1,0:T(8,128)S(1)} %select_multiply_fusion.1, f32[16,16,256]{2,1,0:T(8,128)S(1)} %bitcast_multiply_fusion.1, f32[]{:T(128)} %bitcast.51, f32[]{:T(128)} %bitcast.50, f32[]{:T(128)} %bitcast.49, f32[]{:T(128)} %bitcast.48, f32[]{:T(128)} %bitcast.47, ...), kind=kLoop, calls=%fused_computation.472 | loop fusion | flops 3276800 | bytes 671812 | tf_op jit(solution)/shard_map/convert_element_type | solution.py:161
  100.8 3.9 %collective-permute-start.2 = (bf16[16,8,256]{2,1,0:T(8,128)(2,1)S(1)}, bf16[16,8,256]{2,1,0:T(8,128)(2,1)S(1)}, u32[]{:S(2)}, u32[]{:S(2)}) collective-permute-start(bf16[16,8,256]{2,1,0:T(8,128)(2,1)S(1)} %get-tuple-element.207), channel_id=1, source_target_pairs={{0,32},{32,64},{64,96},{96,128},{128,160},{160,192},{192,224},{224... | collective-permute-start | bytes 196616 | tf_op jit(solution)/shard_map/ppermute | solution.py:32
  106.1 3.6 %collective-permute-done.3 = bf16[16,8,256]{2,1,0:T(8,128)(2,1)S(1)} collective-permute-done((bf16[16,8,256]{2,1,0:T(8,128)(2,1)S(1)}, bf16[16,8,256]{2,1,0:T(8,128)(2,1)S(1)}, u32[]{:S(2)}, u32[]{:S(2)}) %collective-permute-start.3) | collective-permute-done | bytes 65568 | tf_op jit(solution)/shard_map/ppermute | solution.py:34
  109.8 11.4 %fusion.67 = bf16[16,16,256]{2,1,0:T(8,128)(2,1)S(1)} fusion(bf16[16,16,256]{2,1,0:T(8,128)(2,1)S(1)} %copy-done.3, f32[16,16,256]{2,1,0:T(8,128)S(1)} %get-tuple-element.174, f32[16,8,256]{2,1,0:T(8,128)S(1)} %get-tuple-element.200, f32[16,8,256]{2,1,0:T(8,128)S(1)} %get-tuple-element.199, bf16[16,16,256]{2,1,0:T(8,128)(2,1)S(1)} %copy-done.2, ...), kind=kLoop, calls=%fused_computation.183 | loop fusion | flops 3932160 | bytes 917572 | tf_op jit(solution)/shard_map/convert_element_type | solution.py:180
  121.4 51.5 %all_to_all.10 = bf16[16,16,16,256]{3,2,1,0:T(8,128)(2,1)S(1)} all-to-all(bf16[16,16,16,256]{3,2,1,0:T(8,128)(2,1)S(1)} %stack.20), channel_id=1, replica_groups=mesh['segment'=16,'tile'=32] {'segment'}, dimensions={0} | all-to-all | bytes 4194304 | tf_op jit(solution)/shard_map/all_to_all | solution.py:16
  176.0 8.2 %while.21 = (s32[]{:T(128)}, f32[2,8,16,256]{3,2,1,0:T(8,128)}, f32[12,1,31,31]{3,2,0,1:T(8,128)S(1)}, f32[2,8,2,31,31]{4,1,3,2,0:T(8,128)S(1)}, f32[12,1,31,31]...) while((s32[]{:T(128)}, f32[2,8,16,256]{3,2,1,0:T(8,128)}, ...), condition=%wide.region_6.8_spmd, body=%wide.region_4.7_spmd.sunk | while | flops 115241184 | bytes 2505049 | solution.py:118
  176.9 2.6 %multiply_reduce_fusion.5 = f32[8,16,512]{2,1,0:T(8,128)S(1)} fusion(bf16[8,12,31,31]{3,2,1,0:T(8,128)(2,1)S(1)} %get-tuple-element.337, bf16[8,12,31,31]{3,2,1,0:T(8,128)(2,1)S(1)} %fusion.334, bf16[8,12,31,31]{3,2,1,0:T(8,128)(2,1)S(1)} %get-tuple-element.338, bf16[62,512]{1,0:T(8,128)(2,1)} %get-tuple-element.385, ...), kind=kOutput, calls=%fused_computation.31.clone.1 | convolution fusion | flops 113976320 | bytes 881152 | tf_op jit(solution)/shard_map/while/body/eval_jaxpr/nkrb,by->nkry/dot_general | solution.py:109
  181.0 2.6 %multiply_reduce_fusion.5 = f32[8,16,512]{2,1,0:T(8,128)S(1)} fusion(bf16[8,12,31,31]{3,2,1,0:T(8,128)(2,1)S(1)} %get-tuple-element.337, bf16[8,12,31,31]{3,2,1,0:T(8,128)(2,1)S(1)} %fusion.334, bf16[8,12,31,31]{3,2,1,0:T(8,128)(2,1)S(1)} %get-tuple-element.338, bf16[62,512]{1,0:T(8,128)(2,1)} %get-tuple-element.385, ...), kind=kOutput, calls=%fused_computation.31.clone.1 | convolution fusion | flops 113976320 | bytes 881152 | tf_op jit(solution)/shard_map/while/body/eval_jaxpr/nkrb,by->nkry/dot_general | solution.py:109
  185.4 1.9 collective-permute-start.4
  187.3 3.4 %collective-permute-start.5 = (f32[16,16,8]{2,1,0:T(8,128)S(1)}, f32[16,16,8]{2,1,0:T(8,128)S(1)}, u32[]{:S(2)}, u32[]{:S(2)}) collective-permute-start(f32[16,16,8]{2,1,0:T(8,128)S(1)} %get-tuple-element.198), channel_id=1, source_target_pairs={{1,0},{2,1},{3,2},{4,3},{5,4},{6,5},{7,6},{8,7},{9,8},{10,9},{11,1... | collective-permute-start | bytes 24584 | tf_op jit(solution)/shard_map/ppermute | solution.py:22
  192.5 4.2 %collective-permute-done.5 = f32[16,16,8]{2,1,0:T(8,128)S(1)} collective-permute-done((f32[16,16,8]{2,1,0:T(8,128)S(1)}, f32[16,16,8]{2,1,0:T(8,128)S(1)}, u32[]{:S(2)}, u32[]{:S(2)}) %collective-permute-start.5) | collective-permute-done | bytes 8224 | tf_op jit(solution)/shard_map/ppermute | solution.py:22
  197.5 12.2 %fusion.303 = (bf16[16,16,256]{2,1,0:T(8,128)(2,1)S(1)}, f32[16,16,256]{2,1,0:T(8,128)S(1)}) fusion(f32[16,16,8]{2,1,0:T(8,128)S(1)} %select_multiply_fusion, f32[16,16,256]{2,1,0:T(8,128)S(1)} %bitcast_multiply_fusion, f32[]{:T(128)} %bitcast.51, f32[]{:T(128)} %bitcast.50, f32[]{:T(128)} %bitcast.49, f32[]{:T(128)} %bitcast.48, f32[]{:T(128)} %bitcast.47, ...), kind=kLoop, calls=%fused_computation.470 | loop fusion | flops 3276800 | bytes 671812 | tf_op jit(solution)/shard_map/convert_element_type | solution.py:161
  209.7 4.5 %collective-permute-start.6 = (bf16[16,8,256]{2,1,0:T(8,128)(2,1)S(1)}, bf16[16,8,256]{2,1,0:T(8,128)(2,1)S(1)}, u32[]{:S(2)}, u32[]{:S(2)}) collective-permute-start(bf16[16,8,256]{2,1,0:T(8,128)(2,1)S(1)} %get-tuple-element.205), channel_id=1, source_target_pairs={{0,32},{32,64},{64,96},{96,128},{128,160},{160,192},{192,224},{224... | collective-permute-start | bytes 196616 | tf_op jit(solution)/shard_map/ppermute | solution.py:32
  215.6 3.6 %collective-permute-done.7 = bf16[16,8,256]{2,1,0:T(8,128)(2,1)S(1)} collective-permute-done((bf16[16,8,256]{2,1,0:T(8,128)(2,1)S(1)}, bf16[16,8,256]{2,1,0:T(8,128)(2,1)S(1)}, u32[]{:S(2)}, u32[]{:S(2)}) %collective-permute-start.7) | collective-permute-done | bytes 65568 | tf_op jit(solution)/shard_map/ppermute | solution.py:34
  219.3 12.1 %fusion.70 = (bf16[16,16,256]{2,1,0:T(8,128)(2,1)}, f32[16,16,256]{2,1,0:T(8,128)}) fusion(bf16[16,16,256]{2,1,0:T(8,128)(2,1)S(1)} %copy-done.4, bf16[16,16,256]{2,1,0:T(8,128)(2,1)S(1)} %copy-done.1, f32[16,8,256]{2,1,0:T(8,128)S(1)} %get-tuple-element.194, f32[16,16,256]{2,1,0:T(8,128)S(1)} %get-tuple-element.170, f32[]{:T(128)} %bitcast.51, ...), kind=kLoop, calls=%fused_computation.186 | loop fusion | flops 3932160 | bytes 1179716 | tf_op jit(solution)/shard_map/convert_element_type | solution.py:180
  (140 shorter events, 32.8 us)
Async XLA Ops:
  3.1 54.4 %all-to-all-start = ((bf16[16,16,16,256]{3,2,1,0:T(8,128)(2,1)}), bf16[16,16,16,256]{3,2,1,0:T(8,128)(2,1)S(1)}, u32[]{:S(2)}, u32[]{:S(2)}) async-start(bf16[16,16,16,256]{3,2,1,0:T(8,128)(2,1)} %stack.16), calls=%async_computation | async-start | bytes 4194304 | tf_op jit(solution)/shard_map/all_to_all | solution.py:16
  10.7 48.4 %copy-start.6 = (bf16[256,31]{0,1:T(8,128)(2,1)}, bf16[256,31]{0,1:T(8,128)(2,1)S(1)}, u32[]{:S(2)}) copy-start(bf16[256,31]{0,1:T(8,128)(2,1)S(1)} %get-tuple-element.235) | copy-start | bytes 47620
  71.2 17.3 %copy-start.11 = (pred[16]{0:T(512)(128)(4,1)S(1)}, pred[16]{0:T(512)(128)(4,1)}, u32[]{:S(2)}) copy-start(pred[16]{0:T(512)(128)(4,1)} %get-tuple-element.211) | copy-start | bytes 52
  71.2 17.3 %copy-start.14 = (f32[16]{0:T(128)S(1)}, f32[16]{0:T(128)}, u32[]{:S(2)}) copy-start(f32[16]{0:T(128)} %get-tuple-element.210) | copy-start | bytes 196
  72.3 37.4 %copy-start.9 = (f32[16]{0:T(128)S(1)}, f32[16]{0:T(128)}, u32[]{:S(2)}) copy-start(f32[16]{0:T(128)} %get-tuple-element.171) | copy-start | bytes 196
  72.4 8.5 %collective-permute-start = (f32[16,16,8]{2,1,0:T(8,128)S(1)}, f32[16,16,8]{2,1,0:T(8,128)S(1)}, u32[]{:S(2)}, u32[]{:S(2)}) collective-permute-start(f32[16,16,8]{2,1,0:T(8,128)S(1)} %get-tuple-element.203), channel_id=1, source_target_pairs={{0,1},{1,2},{2,3},{3,4},{4,5},{5,6},{6,7},{7,8},{8,9},{9,10},{10,1... | collective-permute-start | bytes 24584 | tf_op jit(solution)/shard_map/ppermute | solution.py:22
  78.2 31.7 %copy-start.8 = (s32[1024]{0:T(1024)}, s32[1024]{0:T(1024)S(1)}, u32[]{:S(2)}) copy-start(s32[1024]{0:T(1024)S(1)} %pad_clamp_fusion) | copy-start | bytes 12292
  78.9 9.0 %collective-permute-start.1 = (f32[16,16,8]{2,1,0:T(8,128)S(1)}, f32[16,16,8]{2,1,0:T(8,128)S(1)}, u32[]{:S(2)}, u32[]{:S(2)}) collective-permute-start(f32[16,16,8]{2,1,0:T(8,128)S(1)} %get-tuple-element.204), channel_id=1, source_target_pairs={{1,0},{2,1},{3,2},{4,3},{5,4},{6,5},{7,6},{8,7},{9,8},{10,9},{11,1... | collective-permute-start | bytes 24584 | tf_op jit(solution)/shard_map/ppermute | solution.py:22
  82.5 27.3 %copy-start.2 = (bf16[16,16,256]{2,1,0:T(8,128)(2,1)S(1)}, bf16[16,16,256]{2,1,0:T(8,128)(2,1)}, u32[]{:S(2)}) copy-start(bf16[16,16,256]{2,1,0:T(8,128)(2,1)} %param.12) | copy-start | bytes 393220
  82.5 27.3 %copy-start.3 = (bf16[16,16,256]{2,1,0:T(8,128)(2,1)S(1)}, bf16[16,16,256]{2,1,0:T(8,128)(2,1)}, u32[]{:S(2)}) copy-start(bf16[16,16,256]{2,1,0:T(8,128)(2,1)} %param.13) | copy-start | bytes 393220
  100.8 5.3 %collective-permute-start.2 = (bf16[16,8,256]{2,1,0:T(8,128)(2,1)S(1)}, bf16[16,8,256]{2,1,0:T(8,128)(2,1)S(1)}, u32[]{:S(2)}, u32[]{:S(2)}) collective-permute-start(bf16[16,8,256]{2,1,0:T(8,128)(2,1)S(1)} %get-tuple-element.207), channel_id=1, source_target_pairs={{0,32},{32,64},{64,96},{96,128},{128,160},{160,192},{192,224},{224... | collective-permute-start | bytes 196616 | tf_op jit(solution)/shard_map/ppermute | solution.py:32
  104.8 4.9 %collective-permute-start.3 = (bf16[16,8,256]{2,1,0:T(8,128)(2,1)S(1)}, bf16[16,8,256]{2,1,0:T(8,128)(2,1)S(1)}, u32[]{:S(2)}, u32[]{:S(2)}) collective-permute-start(bf16[16,8,256]{2,1,0:T(8,128)(2,1)S(1)} %get-tuple-element.208), channel_id=1, source_target_pairs={{32,0},{64,32},{96,64},{128,96},{160,128},{192,160},{224,192},{256... | collective-permute-start | bytes 196616 | tf_op jit(solution)/shard_map/ppermute | solution.py:34
  104.9 16.6 %copy-start.20 = (f32[16]{0:T(128)}, f32[16]{0:T(128)S(1)}, u32[]{:S(2)}) copy-start(f32[16]{0:T(128)S(1)} %add_convert_fusion.2) | copy-start | bytes 196
  121.2 51.8 %copy-start = (bf16[16,16,256]{2,1,0:T(8,128)(2,1)}, bf16[16,16,256]{2,1,0:T(8,128)(2,1)S(1)}, u32[]{:S(2)}) copy-start(bf16[16,16,256]{2,1,0:T(8,128)(2,1)S(1)} %fusion.67) | copy-start | bytes 393220
  176.0 16.2 %copy-start.13 = (pred[16]{0:T(512)(128)(4,1)S(1)}, pred[16]{0:T(512)(128)(4,1)}, u32[]{:S(2)}) copy-start(pred[16]{0:T(512)(128)(4,1)} %get-tuple-element.175) | copy-start | bytes 52
  176.0 16.2 %copy-start.16 = (f32[16]{0:T(128)S(1)}, f32[16]{0:T(128)}, u32[]{:S(2)}) copy-start(f32[16]{0:T(128)} %get-tuple-element.209) | copy-start | bytes 196
  185.4 33.8 %copy-start.10 = (f32[16]{0:T(128)S(1)}, f32[16]{0:T(128)}, u32[]{:S(2)}) copy-start(f32[16]{0:T(128)} %get-tuple-element.171) | copy-start | bytes 196
  185.4 33.8 %copy-start.21 = (f32[16]{0:T(128)S(1)}, f32[16]{0:T(128)}, u32[]{:S(2)}) copy-start(f32[16]{0:T(128)} %copy-done.20) | copy-start | bytes 196
  185.4 6.0 %collective-permute-start.4 = (f32[16,16,8]{2,1,0:T(8,128)S(1)}, f32[16,16,8]{2,1,0:T(8,128)S(1)}, u32[]{:S(2)}, u32[]{:S(2)}) collective-permute-start(f32[16,16,8]{2,1,0:T(8,128)S(1)} %get-tuple-element.197), channel_id=1, source_target_pairs={{0,1},{1,2},{2,3},{3,4},{4,5},{5,6},{6,7},{7,8},{8,9},{9,10},{10,1... | collective-permute-start | bytes 24584 | tf_op jit(solution)/shard_map/ppermute | solution.py:22
  187.3 9.3 %collective-permute-start.5 = (f32[16,16,8]{2,1,0:T(8,128)S(1)}, f32[16,16,8]{2,1,0:T(8,128)S(1)}, u32[]{:S(2)}, u32[]{:S(2)}) collective-permute-start(f32[16,16,8]{2,1,0:T(8,128)S(1)} %get-tuple-element.198), channel_id=1, source_target_pairs={{1,0},{2,1},{3,2},{4,3},{5,4},{6,5},{7,6},{8,7},{9,8},{10,9},{11,1... | collective-permute-start | bytes 24584 | tf_op jit(solution)/shard_map/ppermute | solution.py:22
  192.4 27.0 %copy-start.1 = (bf16[16,16,256]{2,1,0:T(8,128)(2,1)S(1)}, bf16[16,16,256]{2,1,0:T(8,128)(2,1)}, u32[]{:S(2)}) copy-start(bf16[16,16,256]{2,1,0:T(8,128)(2,1)} %copy-done) | copy-start | bytes 393220
  192.4 26.9 %copy-start.4 = (bf16[16,16,256]{2,1,0:T(8,128)(2,1)S(1)}, bf16[16,16,256]{2,1,0:T(8,128)(2,1)}, u32[]{:S(2)}) copy-start(bf16[16,16,256]{2,1,0:T(8,128)(2,1)} %param.13) | copy-start | bytes 393220
  209.7 5.8 %collective-permute-start.6 = (bf16[16,8,256]{2,1,0:T(8,128)(2,1)S(1)}, bf16[16,8,256]{2,1,0:T(8,128)(2,1)S(1)}, u32[]{:S(2)}, u32[]{:S(2)}) collective-permute-start(bf16[16,8,256]{2,1,0:T(8,128)(2,1)S(1)} %get-tuple-element.205), channel_id=1, source_target_pairs={{0,32},{32,64},{64,96},{96,128},{128,160},{160,192},{192,224},{224... | collective-permute-start | bytes 196616 | tf_op jit(solution)/shard_map/ppermute | solution.py:32
  214.2 4.9 %collective-permute-start.7 = (bf16[16,8,256]{2,1,0:T(8,128)(2,1)S(1)}, bf16[16,8,256]{2,1,0:T(8,128)(2,1)S(1)}, u32[]{:S(2)}, u32[]{:S(2)}) collective-permute-start(bf16[16,8,256]{2,1,0:T(8,128)(2,1)S(1)} %get-tuple-element.206), channel_id=1, source_target_pairs={{32,0},{64,32},{96,64},{128,96},{160,128},{192,160},{224,192},{256... | collective-permute-start | bytes 196616 | tf_op jit(solution)/shard_map/ppermute | solution.py:34
  (9 other events, 59.0 us)
